TPU v7x, 32 devices: a whole 2x2x4 slice. The times are simulated.
32 devices in a mesh: row: 8 (over y, x, core), col: 4 (over z).
Axes of the slice: x: 2, y: 2, z: 4, core: 2. Of those that a mesh axis runs over, the one named last changes fastest.
Arguments:
- tokens: bfloat16 [3072, 6144], P('row'), may hold values from -6 to 6
- ln_gain: float32 [6144], replicated, may hold values from 0.1 to 1.9
- qkv_weight: bfloat16 [6144, 3, 3072], P('row', None, 'col'), may hold values from -0.078125 to 0.078125
- q_gain: float32 [24, 128], P('col'), may hold values from 0.4 to 5
- k_gain: float32 [24, 128], P('col'), may hold values from 0.4 to 5
- block_mask: int32 [24, 24, 24], P('col'), may hold values from 0 to 1, as said below
- out_weight: bfloat16 [3072, 6144], P('row', 'col'), may hold values from -0.875 to 0.875
- grad_out: bfloat16 [3072, 6144], P('row', 'col'), may hold values from -6 to 6
Outputs:
- branch_out: bfloat16 [3072, 6144], P('row', 'col')
- out_weight_grad: float32 [3072, 6144], P('row', 'col')
Inputs may be any that keep to these rules, and one draw needn't show every extreme that they name: `block_mask`: entries are 0 or 1; every block sees itself; spectral heads see their spatial window, spatial heads their band group, some heads both, with further blocks scattered at rates that differ by head and by band.
All inputs are finite; a program needn't handle non-finite values.
Results may differ from a plain program's by a relative error of at most 0.014.
The roundings to bfloat16 on the way count: a program that leaves them out, or rounds other values in their place, can miss the bound.
Values may be sent and summed in bfloat16 or wider, within the bound.
A program may use at most 128 MiB of HBM per device.

v0:
```python
import jax
import jax.numpy as jnp
from jax import lax
from jax.sharding import PartitionSpec as P

HS = 128
BLOCK = 128


EPS = 1e-06


def norm_rows(values, gain):
    center = jnp.mean(values, axis=-1, keepdims=True)
    shifted = values - center
    variance = jnp.mean(shifted * shifted, axis=-1, keepdims=True)
    return shifted * lax.rsqrt(variance + EPS) * gain


def per_device(tokens, ln_gain, qkv_weight, q_gain, k_gain, block_mask, out_weight, grad_out):
    tok_rows = tokens.shape[0]
    heads_here = q_gain.shape[0]
    col_width = heads_here * HS
    normed = norm_rows(tokens.astype(jnp.float32), ln_gain).astype(jnp.bfloat16)
    portion = lax.all_gather(qkv_weight, "row", axis=0, tiled=True)
    columns = normed
    flat_part = portion.reshape(portion.shape[0], 3 * col_width)
    mixed = jnp.dot(columns, flat_part, preferred_element_type=jnp.float32)
    mixed = mixed.reshape(tok_rows, 3, heads_here, HS)
    queries = norm_rows(mixed[:, 0], q_gain).astype(jnp.bfloat16)
    keys_here = norm_rows(mixed[:, 1], k_gain).astype(jnp.bfloat16)
    values_here = mixed[:, 2].astype(jnp.bfloat16)
    nblocks = block_mask.shape[1]
    qblocks = tok_rows // BLOCK
    first_block = lax.axis_index("row") * qblocks
    mask_rows = lax.dynamic_slice_in_dim(block_mask, first_block, qblocks, 1).astype(jnp.float32)
    block_ids = jnp.arange(nblocks, dtype=jnp.int32)
    query_blocks = queries.reshape(qblocks, BLOCK, heads_here, HS)
    score_scale = HS ** (-0.5)
    top_score = jnp.full((heads_here, qblocks, BLOCK), -1e30, jnp.float32)
    key_part = lax.all_gather(keys_here, "row", axis=0, tiled=True)
    value_part = lax.all_gather(values_here, "row", axis=0, tiled=True)
    count_keys = key_part.shape[0]
    scores = (
        jnp.einsum("abhd,khd->habk", query_blocks, key_part, preferred_element_type=jnp.float32)
        * score_scale
    )
    owner = jnp.arange(count_keys, dtype=jnp.int32) // BLOCK
    one_hot = (owner[:, None] == block_ids[None, :]).astype(jnp.float32)
    allowed = jnp.einsum("haj,kj->hak", mask_rows, one_hot)
    is_live = allowed[:, :, None, :] > 0.5
    scores = jnp.where(is_live, scores, -1e30)
    new_top = jnp.maximum(top_score, jnp.max(scores, axis=-1))
    expo = jnp.where(is_live, jnp.exp(scores - new_top[..., None]), 0.0)
    denom = jnp.sum(expo, axis=-1)
    product = jnp.einsum(
        "habk,khd->habd", expo.astype(jnp.bfloat16), value_part, preferred_element_type=jnp.float32
    )
    accum = product
    top_score, denom, accum = (new_top, denom, accum)
    attn_here = (accum / denom[..., None]).astype(jnp.bfloat16)
    attn_here = attn_here.transpose(1, 2, 0, 3).reshape(tok_rows, col_width)
    whole_attn = lax.all_gather(attn_here, "col", axis=1, tiled=True)
    columns = whole_attn
    branch = jnp.dot(
        columns,
        lax.all_gather(out_weight, "row", axis=0, tiled=True),
        preferred_element_type=jnp.float32,
    )
    columns = whole_attn
    weight_grad = lax.psum_scatter(
        jnp.einsum("tk,td->kd", columns, grad_out, preferred_element_type=jnp.float32).astype(
            jnp.bfloat16
        ),
        "row",
        scatter_dimension=0,
        tiled=True,
    ).astype(jnp.float32)
    return (branch.astype(jnp.bfloat16), weight_grad)


def solution(mesh):
    in_specs = (
        P("row", None),
        P(),
        P("row", None, "col"),
        P("col", None),
        P("col", None),
        P("col", None, None),
        P("row", "col"),
        P("row", "col"),
    )
    out_specs = (P("row", "col"), P("row", "col"))
    return jax.shard_map(
        per_device, mesh=mesh, in_specs=in_specs, out_specs=out_specs, check_vma=False
    )
```

profile of v0, /device:TPU:0, one launch (start us, length us, event | category | flops | bytes accessed | tf_op | source)
XLA Modules:
  0.0 469.9 jit_solution(9573965271223659593)
XLA Ops:
  7.2 0.0 copy-start
  7.2 0.0 all-gather.7.cloned.1.call-start
  7.2 6.1 %copy.14 = bf16[768,3,768]{0,2,1:T(8,128)(2,1)} copy(bf16[768,3,768]{2,0,1:T(8,128)(2,1)} %param.10) | data formatting | bytes 7077888 | tf_op args[2]
  13.4 0.0 all-gather.7.cloned.1.call-update
  13.4 0.0 copy-start.5
  13.4 0.0 all-gather.9.cloned.1.call-start
  13.5 3.0 convert_reduce_fusion
  16.5 3.7 fusion.8
  20.2 134.0 %all-gather.7.cloned.1.call-done = bf16[6144,3,768]{0,2,1:T(8,128)(2,1)} async-done(((bf16[768,3,768]{0,2,1:T(8,128)(2,1)}), bf16[6144,3,768]{0,2,1:T(8,128)(2,1)}) %all-gather.7.cloned.1.call-update) | async-done | bytes 28311568 | tf_op jit(solution)/shard_map/all_gather | solution.py:25
  154.2 0.0 copy-done.5
  154.3 16.1 %fusion.12 = f32[384,3,6,128]{3,0,2,1:T(8,128)S(1)} fusion(bf16[3,6,128,6144]{3,2,1,0:T(8,128)(2,1)} %bitcast.66, bf16[384,6144]{1,0:T(8,128)(2,1)} %param.8, f32[6144]{0:T(1024)S(1)} %copy-done.5, f32[384]{0:T(512)S(1)} %add_rsqrt_fusion.2, f32[384]{0:T(512)S(1)} %broadcast_multiply_fusion.2), kind=kOutput, calls=%fused_computation.16 | convolution fusion | flops 10883432448 | bytes 36596736 | tf_op jit(solution)/shard_map/dot_general | solution.py:28
  170.3 0.0 copy-start.1
  170.4 0.0 copy-start.3
  170.4 0.0 copy-start.2
  170.4 0.7 slice_reduce_fusion.1
  171.1 1.4 fusion.26
  172.5 0.0 copy-done.1
  172.6 0.0 copy-done.3
  172.6 1.5 multiply_convert_fusion
  174.1 0.0 all-gather.9.cloned.1.call-update
  174.1 0.0 all-gather.15.cloned.1.call-start
  174.1 2.2 slice.22
  176.3 0.0 all-gather.15.cloned.1.call-update
  176.3 0.2 all-gather.11.cloned.1.call-start
  176.6 0.8 constant_dynamic-slice_fusion
  177.4 0.2 convolution_compare_fusion
  177.6 0.1 copy.13
  177.7 35.4 %all-gather.9.cloned.1.call-done = bf16[3072,6,128]{2,0,1:T(8,128)(2,1)} async-done(((bf16[384,6,128]{2,0,1:T(8,128)(2,1)}), bf16[3072,6,128]{2,0,1:T(8,128)(2,1)}) %all-gather.9.cloned.1.call-update) | async-done | bytes 4718608 | tf_op jit(solution)/shard_map/all_gather | solution.py:41
  213.2 0.0 copy-done.2
  213.2 13.6 %fusion = (f32[6,3,128]{2,1,0:T(4,128)S(1)}, f32[6,3,128,3072]{3,2,1,0:T(8,128)}) fusion(pred[6,3,3072]{2,1,0:T(4,128)(4,1)S(1)} %copy.13, bf16[3072,6,128]{2,0,1:T(8,128)(2,1)} %all-gather.9.cloned.1.call-done, f32[3,128,6,128]{3,1,0,2:T(8,128)S(1)} %bitcast.62, f32[6,128]{1,0:T(8,128)S(1)} %copy-done.2, f32[3,128,6]{1,0,2:T(4,128)S(1)} %rsqrt.29, ...), kind=kOutput, calls=%fused_computation.2 | convolution fusion | flops 1834350336 | bytes 34295808 | tf_op jit(solution)/shard_map/abhd,khd->habk/dot_general | solution.py:45
  226.7 13.0 %fusion.1 = f32[6,3,128]{2,1,0:T(4,128)S(1)} fusion(f32[6,3,128,3072]{3,2,1,0:T(8,128)} %get-tuple-element.8, f32[6,3,128]{2,1,0:T(4,128)S(1)} %broadcast_maximum_fusion, pred[6,3,3072]{2,1,0:T(4,128)(4,1)S(1)} %copy.13), kind=kLoop, calls=%fused_computation.3 | loop fusion | flops 35387136 | bytes 28385280 | tf_op jit(solution)/shard_map/reduce_sum | solution.py:55
  239.8 14.8 %all-gather.15.cloned.1.call-done = bf16[3072,1,6,128]{3,0,2,1:T(8,128)(2,1)} async-done(((bf16[384,1,6,128]{3,0,2,1:T(8,128)(2,1)}), bf16[3072,1,6,128]{3,0,2,1:T(8,128)(2,1)}) %all-gather.15.cloned.1.call-update) | async-done | bytes 4718608 | tf_op jit(solution)/shard_map/all_gather | solution.py:42
  254.6 14.2 %divide_convert_fusion = bf16[3,128,6,128]{3,1,0,2:T(8,128)(2,1)S(1)} fusion(bf16[3072,1,6,128]{3,0,2,1:T(8,128)(2,1)} %all-gather.15.cloned.1.call-done, f32[6,3,128,3072]{3,2,1,0:T(8,128)} %get-tuple-element.8, f32[6,3,128]{2,1,0:T(4,128)S(1)} %broadcast_maximum_fusion, pred[6,3,3072]{2,1,0:T(4,128)(4,1)S(1)} %copy.13, f32[3,128,6]{1,0,2:T(4,128)S(1)} %bitcast.65), kind=kOutput, calls=%fused_computation.31 | convolution fusion | flops 1847918592 | bytes 33693696 | tf_op jit(solution)/shard_map/habk,khd->habd/dot_general | solution.py:56
  268.8 0.4 copy.15
  269.2 0.9 copy.24
  270.1 0.0 all-gather.11.cloned.1.call-update
  270.1 0.0 all-gather.13.cloned.1.call-start
  270.2 0.5 all-gather.13.cloned.1.call-update
  270.7 0.0 reduce-scatter.2.cloned.1.call-start
  270.8 50.0 %all-gather.11.cloned.1.call-done = bf16[384,3072]{1,0:T(8,128)(2,1)} async-done(((bf16[384,768]{1,0:T(8,128)(2,1)}), bf16[384,3072]{1,0:T(8,128)(2,1)}) %all-gather.11.cloned.1.call-update) | async-done | bytes 2359312 | tf_op jit(solution)/shard_map/all_gather | solution.py:63
  320.7 0.0 copy-done
  320.7 9.3 %convolution_convert_fusion = bf16[3072,1536]{1,0:T(8,128)(2,1)} fusion(bf16[384,3072]{1,0:T(8,128)(2,1)} %all-gather.11.cloned.1.call-done, bf16[384,1536]{1,0:T(8,128)(2,1)S(1)} %copy-done), kind=kOutput, calls=%fused_computation.9 | convolution fusion | flops 3628597248 | bytes 12976128 | tf_op jit(solution)/shard_map/tk,td->kd/dot_general | solution.py:72
  330.0 0.0 copy-start.4
  330.0 0.0 reduce-scatter.2.cloned.1.call-update
  330.0 50.1 %all-gather.13.cloned.1.call-done = bf16[3072,1536]{1,0:T(8,128)(2,1)} async-done(((bf16[384,1536]{1,0:T(8,128)(2,1)}), bf16[3072,1536]{1,0:T(8,128)(2,1)}) %all-gather.13.cloned.1.call-update) | async-done | bytes 9437200 | tf_op jit(solution)/shard_map/all_gather | solution.py:67
  380.2 0.0 copy-done.4
  380.2 7.5 %convolution_convert_fusion.1 = bf16[384,1536]{1,0:T(8,128)(2,1)} fusion(bf16[384,3072]{1,0:T(8,128)(2,1)S(1)} %copy-done.4, bf16[3072,1536]{1,0:T(8,128)(2,1)} %all-gather.13.cloned.1.call-done), kind=kOutput, calls=%fused_computation.24 | convolution fusion | flops 3624468480 | bytes 12976128 | tf_op jit(solution)/shard_map/dot_general | solution.py:65
  387.6 72.4 %reduce-scatter.2.cloned.1.call-done = bf16[384,1536]{1,0:T(8,128)(2,1)} async-done(((bf16[3072,1536]{1,0:T(8,128)(2,1)}), bf16[384,1536]{1,0:T(8,128)(2,1)}) %reduce-scatter.2.cloned.1.call-update) | async-done | bytes 1179664 | tf_op jit(solution)/shard_map/reduce_scatter | solution.py:71
  460.0 3.0 convert_element_type.47
  (9 shorter events, 0.1 us)
Async XLA Ops:
  7.2 313.6 %copy-start = (bf16[384,1536]{1,0:T(8,128)(2,1)S(1)}, bf16[384,1536]{1,0:T(8,128)(2,1)}, u32[]{:S(2)}) copy-start(bf16[384,1536]{1,0:T(8,128)(2,1)} %param.15) | copy-start | bytes 3538948
  7.2 147.1 %all-gather.7.cloned.1.call-start = ((), (), s32[]{:S(2)}) async-start(), calls=%async_computation.1 | async-start | bytes 31850496 | tf_op jit(solution)/shard_map/all_gather | solution.py:25
  13.4 140.9 %copy-start.5 = (f32[6144]{0:T(1024)S(1)}, f32[6144]{0:T(1024)}, u32[]{:S(2)}) copy-start(f32[6144]{0:T(1024)} %param.9) | copy-start | bytes 73732
  13.4 199.8 %all-gather.9.cloned.1.call-start = ((), (), s32[]{:S(2)}) async-start(), calls=%async_computation.2 | async-start | bytes 5308416 | tf_op jit(solution)/shard_map/all_gather | solution.py:41
  170.3 2.2 copy-start.1
  170.4 2.2 copy-start.3
  170.4 42.8 %copy-start.2 = (f32[6,128]{1,0:T(8,128)S(1)}, f32[6,128]{1,0:T(8,128)}, u32[]{:S(2)}) copy-start(f32[6,128]{1,0:T(8,128)} %param.11) | copy-start | bytes 9220
  174.1 80.5 %all-gather.15.cloned.1.call-start = ((), (), s32[]{:S(2)}) async-start(), calls=%async_computation.6 | async-start | bytes 5308416 | tf_op jit(solution)/shard_map/all_gather | solution.py:42
  176.3 144.4 %all-gather.11.cloned.1.call-start = ((), (), s32[]{:S(2)}) async-start(), calls=%async_computation.3 | async-start | bytes 2949120 | tf_op jit(solution)/shard_map/all_gather | solution.py:63
  270.1 110.0 %all-gather.13.cloned.1.call-start = ((), (), s32[]{:S(2)}) async-start(), calls=%async_computation.4 | async-start | bytes 10616832 | tf_op jit(solution)/shard_map/all_gather | solution.py:67
  270.7 189.3 %reduce-scatter.2.cloned.1.call-start = ((), (), s32[]{:S(2)}) async-start(), calls=%async_computation.5 | async-start | bytes 10616832 | tf_op jit(solution)/shard_map/reduce_scatter | solution.py:71
  330.0 50.2 %copy-start.4 = (bf16[384,3072]{1,0:T(8,128)(2,1)S(1)}, bf16[384,3072]{1,0:T(8,128)(2,1)}, u32[]{:S(2)}) copy-start(bf16[384,3072]{1,0:T(8,128)(2,1)} %all-gather.11.cloned.1.call-done) | copy-start | bytes 7077892
Sparse Core Ops, SparseCore 0:
  13.5 140.6 all-gather.6
  174.2 38.9 all-gather.8
  215.6 38.9 all-gather.14
  270.2 50.4 all-gather.10
  322.4 57.6 all-gather.12
  383.5 76.4 reduce-scatter.1
where the time goes:
time: 470 us
  waiting for transfers between devices  357 us (76%)
  matrix products  60.8 us (13%)
  other arithmetic  26.4 us (6%)
  between operations  14.3 us (3%)
  local copies, waits for them, and re-layouts  10.6 us (2%)
    all_gather x1, waiting for transfers between devices, per_device(): portion = lax.all_gather(qkv_weight, 'row', axis=0, tiled=True)  134 us
    reduce_scatter x1, waiting for transfers between devices, per_device(): lax.psum_scatter(jnp.einsum('tk,td->kd', columns, grad_out, preferred_ele...  72.4 us
    all_gather x1, waiting for transfers between devices, per_device(): lax.all_gather(out_weight, 'row', axis=0, tiled=True)  50.1 us
    all_gather x1, waiting for transfers between devices, per_device(): whole_attn = lax.all_gather(attn_here, 'col', axis=1, tiled=True)  50 us
    all_gather x1, waiting for transfers between devices, per_device(): key_part = lax.all_gather(keys_here, 'row', axis=0, tiled=True)  35.4 us
    dot_general x1, matrix products, per_device(): mixed = jnp.dot(columns, flat_part, preferred_element_type=jnp.float32)  16.1 us
    all_gather x1, waiting for transfers between devices, per_device(): value_part = lax.all_gather(values_here, 'row', axis=0, tiled=True)  14.8 us
    dot_general x1, matrix products, per_device(): jnp.einsum('habk,khd->habd', expo.astype(jnp.bfloat16), value_part, prefe...  14.2 us
  transfers between devices with their start and end apart: 6, of which 6 were waited for; matrix products, arithmetic and copies ran while one was open for 11% of the time, Pallas kernels for 0%

commit v1 on v0

v1 whole, which is shorter than its diff:
```python
import functools

import jax
import jax.numpy as jnp
from jax import lax
from jax.experimental import pallas as pl
from jax.experimental.pallas import tpu as pltpu
from jax.sharding import PartitionSpec as P

HS = 128
BLOCK = 128
EPS = 1e-06
MESH = pl.DeviceIdType.MESH
SUBS = 2


def norm_rows(values, gain):
    center = jnp.mean(values, axis=-1, keepdims=True)
    shifted = values - center
    variance = jnp.mean(shifted * shifted, axis=-1, keepdims=True)
    return shifted * lax.rsqrt(variance + EPS) * gain


def flip(index, bit):
    return index + bit - 2 * bit * ((index // bit) % 2)


def places():
    row, col = lax.axis_index("row"), lax.axis_index("col")
    return row, col, flip(row, 1), flip(row, 2), flip(row, 4), flip(flip(row, 2), 4)


def remote(src, dst, send, recv, device):
    return pltpu.make_async_remote_copy(
        src_ref=src, dst_ref=dst, send_sem=send, recv_sem=recv, device_id=device, device_id_type=MESH
    )


def project_kernel(ncol, tok_ref, w_ref, qg_ref, kg_ref, out_ref, wbuf, tbuf, acc,
                   w_recv, w_send, t_recv, t_send):
    row, col, mate, xn, yn, dn = places()
    half = (row // 2) % 2
    rows_tok, depth = tok_ref.shape[1], tok_ref.shape[2]
    per = tok_ref.shape[0] // ncol
    width = w_ref.shape[-1]
    tile = width // 3
    sub = depth // SUBS

    barrier = pltpu.get_barrier_semaphore()
    for other in (mate, xn, yn):
        pl.semaphore_signal(barrier, inc=1, device_id=(other, col), device_id_type=MESH)

    @pl.when(col > 0)
    def _():
        pl.semaphore_signal(barrier, inc=1, device_id=(row, col - 1), device_id_type=MESH)

    @pl.when(col < ncol - 1)
    def _():
        pl.semaphore_signal(barrier, inc=1, device_id=(row, col + 1), device_id_type=MESH)

    pl.semaphore_wait(barrier, 3 + jnp.where(col > 0, 1, 0) + jnp.where(col < ncol - 1, 1, 0))

    def wpart(block, s):
        return wbuf.at[block, pl.ds(s * sub, sub)]

    def wown(which, s):
        return w_ref.at[which, pl.ds(s * sub, sub)]

    def wcopy(src, block, s, slot, device):
        return remote(src, wpart(block, s), w_send.at[slot, s], w_recv.at[block, s], (device, col))

    def tcopy(src, block, q, slot, device):
        return remote(src, tbuf.at[block], t_send.at[slot, q], t_recv.at[block], device)

    first = [tcopy(tok_ref.at[col * per + q], col * per + q, q, 0, (xn, col)) for q in range(per)]
    for copy in first:
        copy.start()
    to_y = [wcopy(wown(half, s), row, s, 0, yn) for s in range(SUBS)]
    to_x = [wcopy(wown(1 - half, s), row, s, 1, xn) for s in range(SUBS)]
    to_mate = [wcopy(wown(half, s), row, s, 2, mate) for s in range(SUBS)]
    for copy in to_y + to_mate:
        copy.start()

    own_at = pl.multiple_of(half * rows_tok, rows_tok)
    nbr_at = pl.multiple_of((1 - half) * rows_tok, rows_tok)

    def times(at, left, right, fresh):
        @pl.loop(0, 3)
        def _(t):
            cols = pl.ds(pl.multiple_of(t * tile, tile), tile)
            prod = jnp.dot(left[...], right[:, cols], preferred_element_type=jnp.float32)
            if fresh:
                acc[pl.ds(at, rows_tok), cols] = prod
            else:
                acc[pl.ds(at, rows_tok), cols] += prod

    times(own_at, tok_ref.at[row], w_ref.at[half], True)

    def up(block, q, slot):
        return tcopy(tbuf.at[block], block, q, slot, (row, col + 1))

    def down(block, q, slot):
        return tcopy(tbuf.at[block], block, q, slot, (row, col - 1))

    def t_got(block):
        tcopy(tbuf.at[block], block, 0, 0, (xn, col)).wait_recv()

    def w_got(block, s):
        wcopy(wpart(block, s), block, s, 0, xn).wait_recv()

    def spread(dist, q):
        if dist == 0:
            block = col * per + q
            t_got(block)

            @pl.when(col < ncol - 1)
            def _():
                up(block, q, 1).start()

            @pl.when(col > 0)
            def _():
                down(block, q, 2).start()
            return

        @pl.when(col >= dist)
        def _():
            block = (col - dist) * per + q
            t_got(block)

            @pl.when(col < ncol - 1)
            def _():
                up(block, q, 2 * dist + 1).start()

        @pl.when(col + dist < ncol)
        def _():
            block = (col + dist) * per + q
            t_got(block)

            @pl.when(col > 0)
            def _():
                down(block, q, 2 * dist + 2).start()

    pend = []

    def pass_w(block, s, slots):
        w_got(block, s)
        for slot, device in slots:
            copy = wcopy(wpart(block, s), block, s, slot, device)
            copy.start()
            pend.append(copy)

    for q in range(per):
        spread(0, q)
    for copy in to_x:
        copy.start()
    pass_w(yn, 0, [(3, mate)])
    spread(1, 0)
    pass_w(yn, 1, [(3, mate)])
    spread(1, 1)
    times(own_at, tok_ref.at[yn], wbuf.at[yn], False)
    pass_w(xn, 0, [(4, yn), (5, mate)])
    spread(2, 0)
    pass_w(xn, 1, [(4, yn), (5, mate)])
    spread(2, 1)
    times(own_at, tok_ref.at[xn], wbuf.at[xn], False)
    for block in (mate, flip(mate, 4), flip(mate, 2)):
        for s in range(SUBS):
            w_got(block, s)
        times(own_at, tok_ref.at[block], wbuf.at[block], False)
    for s in range(SUBS):
        pass_w(dn, s, [(6, mate)])
    times(own_at, tok_ref.at[dn], wbuf.at[dn], False)
    for dist in range(3, ncol):
        for q in range(per):
            spread(dist, q)
    times(nbr_at, tbuf.at[row], w_ref.at[half], True)
    for block in (mate, flip(mate, 4), flip(mate, 2), yn, xn, dn):
        times(nbr_at, tbuf.at[block], wbuf.at[block], False)
    last = flip(dn, 1)
    for s in range(SUBS):
        w_got(last, s)
    times(own_at, tok_ref.at[last], wbuf.at[last], False)
    times(nbr_at, tbuf.at[last], wbuf.at[last], False)

    heads = qg_ref.shape[0]
    for kind in range(3):
        for h in range(heads):
            at = (kind * heads + h) * HS
            part = acc[:, at:at + HS]
            if kind < 2:
                part = norm_rows(part, (qg_ref, kg_ref)[kind][h:h + 1, :])
            out_ref[kind, h] = part.astype(jnp.bfloat16)

    for copy in first + to_y + to_x + to_mate + pend:
        copy.wait_send()
    for q in range(per):
        for dist in range(ncol):
            @pl.when((col >= dist) & (col < ncol - 1))
            def _():
                block = (col - dist) * per + q
                up(block, q, 2 * dist + 1).wait_send()

            @pl.when((col + dist < ncol) & (col > 0))
            def _():
                block = (col + dist) * per + q
                down(block, q, 2 * dist + 2).wait_send()


def attend_kernel(qkv_ref, bias_ref, out_ref, kvbuf, recv, send):
    row, col, mate, xn, yn, dn = places()
    heads, rows = qkv_ref.shape[1], qkv_ref.shape[2]
    here = 2 * (row // 4) + row % 2
    yslot = flip(here, 2)
    barrier = pltpu.get_barrier_semaphore()
    for other in (mate, yn):
        pl.semaphore_signal(barrier, inc=1, device_id=(other, col), device_id_type=MESH)
    pl.semaphore_wait(barrier, 2)

    def copy(src, kv, h, slot, way, device):
        return remote(src, kvbuf.at[kv, h, slot], send.at[way, kv, h], recv.at[kv, h, slot], (device, col))

    started = []
    for h in range(heads):
        for kv in range(2):
            for way, device in ((0, yn), (1, mate)):
                one = copy(qkv_ref.at[1 + kv, h], kv, h, here, way, device)
                one.start()
                started.append(one)
            kvbuf[kv, h, here] = qkv_ref[1 + kv, h]
    scale = HS ** (-0.5)
    for h in range(heads):
        for kv in range(2):
            copy(kvbuf.at[kv, h, yslot], kv, h, yslot, 2, mate).wait_recv()
            one = copy(kvbuf.at[kv, h, yslot], kv, h, yslot, 2, mate)
            one.start()
            started.append(one)
    for h in range(heads):
        for kv in range(2):
            copy(kvbuf.at[kv, h, 0], kv, h, flip(here, 1), 2, mate).wait_recv()
            copy(kvbuf.at[kv, h, 0], kv, h, flip(yslot, 1), 2, mate).wait_recv()

        @pl.loop(0, rows // BLOCK)
        def _(b):
            at = pl.ds(pl.multiple_of(b * BLOCK, BLOCK), BLOCK)
            keys = kvbuf[0, h].reshape(4 * rows, HS)
            scores = lax.dot_general(qkv_ref[0, h, at, :], keys, (((1,), (1,)), ((), ())),
                                     preferred_element_type=jnp.float32) * scale
            scores = scores + bias_ref[h, b]
            top = jnp.max(scores, axis=-1, keepdims=True)
            expo = jnp.exp(scores - top)
            denom = jnp.sum(expo, axis=-1, keepdims=True)
            prod = jnp.dot(expo.astype(jnp.bfloat16), kvbuf[1, h].reshape(4 * rows, HS),
                           preferred_element_type=jnp.float32)
            out_ref[at, h * HS:(h + 1) * HS] = (prod / denom).astype(jnp.bfloat16)
    for one in started:
        one.wait_send()


def vmem(count):
    return [pl.BlockSpec(memory_space=pltpu.VMEM)] * count


def attention_fast(ncol, nrow, tokens, ln_gain, qkv_weight, q_gain, k_gain, block_mask):
    tok_rows, feats = tokens.shape
    depth, _, col_width = qkv_weight.shape
    heads = q_gain.shape[0] // 2
    row = lax.axis_index("row")
    half = (row // 2) % 2
    normed = norm_rows(tokens.astype(jnp.float32), ln_gain).astype(jnp.bfloat16)
    normed = normed.reshape(tok_rows, nrow, depth).transpose(1, 0, 2)
    wide = 3 * heads * HS
    weight = qkv_weight.reshape(depth, 3, 2, heads * HS).transpose(2, 0, 1, 3).reshape(2, depth, wide)
    qg = lax.dynamic_slice_in_dim(q_gain, half * heads, heads, 0)
    kg = lax.dynamic_slice_in_dim(k_gain, half * heads, heads, 0)
    dma = pltpu.SemaphoreType.DMA
    qkv = pl.pallas_call(
        functools.partial(project_kernel, ncol),
        out_shape=jax.ShapeDtypeStruct((3, heads, 2 * tok_rows, HS), jnp.bfloat16),
        in_specs=vmem(4),
        out_specs=vmem(1)[0],
        scratch_shapes=[
            pltpu.VMEM((nrow, depth, wide), jnp.bfloat16),
            pltpu.VMEM((nrow, tok_rows, depth), jnp.bfloat16),
            pltpu.VMEM((2 * tok_rows, wide), jnp.float32),
            dma((nrow, SUBS)), dma((7, SUBS)), dma((nrow,)), dma((2 * ncol + 1, nrow // ncol)),
        ],
        compiler_params=pltpu.CompilerParams(
            collective_id=0, has_side_effects=True, vmem_limit_bytes=56 * 2**20),
        name="project",
    )(normed, weight, qg, kg)

    per = tok_rows // BLOCK
    nblocks = block_mask.shape[1]
    mask = lax.dynamic_slice_in_dim(block_mask, half * heads, heads, 0)
    order = mask.reshape(heads, 2, 2, 2, per, 2, 2, 2, per)
    mine = lax.dynamic_index_in_dim(order, row // 4, 1, False)
    mine = lax.dynamic_index_in_dim(mine, row % 2, 2, False)
    mine = mine.transpose(0, 1, 2, 3, 5, 4, 6).reshape(heads, 2 * per, nblocks)
    bias = jnp.where(mine > 0, 0.0, -1e30).astype(jnp.float32)
    bias = jnp.repeat(bias, BLOCK, axis=2).reshape(heads, 2 * per, 1, nblocks * BLOCK)
    return pl.pallas_call(
        attend_kernel,
        out_shape=jax.ShapeDtypeStruct((2 * tok_rows, heads * HS), jnp.bfloat16),
        in_specs=vmem(2),
        out_specs=vmem(1)[0],
        scratch_shapes=[
            pltpu.VMEM((2, heads, 4, 2 * tok_rows, HS), jnp.bfloat16),
            dma((2, heads, 4)), dma((3, 2, heads)),
        ],
        compiler_params=pltpu.CompilerParams(
            collective_id=1, has_side_effects=True, vmem_limit_bytes=48 * 2**20),
        name="attend",
    )(qkv, bias)


def fast_device(ncol, nrow, tokens, ln_gain, qkv_weight, q_gain, k_gain, block_mask, out_weight, grad_out):
    tok_rows = tokens.shape[0]
    row = lax.axis_index("row")
    half = (row // 2) % 2
    attn = attention_fast(ncol, nrow, tokens, ln_gain, qkv_weight, q_gain, k_gain, block_mask)
    out_weight, attn = lax.optimization_barrier((out_weight, attn))
    weight_all = lax.all_gather(out_weight, "row", axis=0, tiled=True)
    own = lax.dynamic_slice_in_dim(attn, half * tok_rows, tok_rows, 0)
    give = lax.dynamic_slice_in_dim(attn, (1 - half) * tok_rows, tok_rows, 0)
    got = lax.ppermute(give, "row", [(i, i ^ 2) for i in range(nrow)])
    first = jnp.where(half == 0, own, got)
    second = jnp.where(half == 0, got, own)
    attn_here = jnp.concatenate([first, second], axis=1)
    whole_attn = lax.all_gather(attn_here, "col", axis=1, tiled=True)
    partial = jnp.einsum("tk,td->kd", whole_attn, grad_out, preferred_element_type=jnp.float32)
    weight_grad = lax.psum_scatter(
        partial.astype(jnp.bfloat16), "row", scatter_dimension=0, tiled=True
    ).astype(jnp.float32)
    branch = jnp.dot(whole_attn, weight_all, preferred_element_type=jnp.float32)
    return branch.astype(jnp.bfloat16), weight_grad


def per_device(tokens, ln_gain, qkv_weight, q_gain, k_gain, block_mask, out_weight, grad_out):
    tok_rows = tokens.shape[0]
    heads_here = q_gain.shape[0]
    col_width = heads_here * HS
    normed = norm_rows(tokens.astype(jnp.float32), ln_gain).astype(jnp.bfloat16)
    portion = lax.all_gather(qkv_weight, "row", axis=0, tiled=True)
    flat_part = portion.reshape(portion.shape[0], 3 * col_width)
    mixed = jnp.dot(normed, flat_part, preferred_element_type=jnp.float32)
    mixed = mixed.reshape(tok_rows, 3, heads_here, HS)
    queries = norm_rows(mixed[:, 0], q_gain).astype(jnp.bfloat16)
    keys_here = norm_rows(mixed[:, 1], k_gain).astype(jnp.bfloat16)
    values_here = mixed[:, 2].astype(jnp.bfloat16)
    nblocks = block_mask.shape[1]
    qblocks = tok_rows // BLOCK
    first_block = lax.axis_index("row") * qblocks
    mask_rows = lax.dynamic_slice_in_dim(block_mask, first_block, qblocks, 1)
    query_blocks = queries.reshape(qblocks, BLOCK, heads_here, HS)
    key_part = lax.all_gather(keys_here, "row", axis=0, tiled=True)
    value_part = lax.all_gather(values_here, "row", axis=0, tiled=True)
    scores = (
        jnp.einsum("abhd,khd->habk", query_blocks, key_part, preferred_element_type=jnp.float32)
        * HS ** (-0.5)
    )
    is_live = jnp.repeat(mask_rows > 0, BLOCK, axis=2)[:, :, None, :]
    scores = jnp.where(is_live, scores, -1e30)
    top = jnp.max(scores, axis=-1, keepdims=True)
    expo = jnp.where(is_live, jnp.exp(scores - top), 0.0)
    denom = jnp.sum(expo, axis=-1)
    accum = jnp.einsum(
        "habk,khd->habd", expo.astype(jnp.bfloat16), value_part, preferred_element_type=jnp.float32
    )
    attn_here = (accum / denom[..., None]).astype(jnp.bfloat16)
    attn_here = attn_here.transpose(1, 2, 0, 3).reshape(tok_rows, col_width)
    whole_attn = lax.all_gather(attn_here, "col", axis=1, tiled=True)
    branch = jnp.dot(
        whole_attn,
        lax.all_gather(out_weight, "row", axis=0, tiled=True),
        preferred_element_type=jnp.float32,
    )
    weight_grad = lax.psum_scatter(
        jnp.einsum("tk,td->kd", whole_attn, grad_out, preferred_element_type=jnp.float32).astype(
            jnp.bfloat16
        ),
        "row",
        scatter_dimension=0,
        tiled=True,
    ).astype(jnp.float32)
    return (branch.astype(jnp.bfloat16), weight_grad)


def solution(mesh):
    in_specs = (
        P("row", None),
        P(),
        P("row", None, "col"),
        P("col", None),
        P("col", None),
        P("col", None, None),
        P("row", "col"),
        P("row", "col"),
    )
    out_specs = (P("row", "col"), P("row", "col"))
    nrow, ncol = mesh.shape["row"], mesh.shape["col"]
    body = per_device
    if (nrow, ncol) == (8, 4):
        body = functools.partial(fast_device, ncol, nrow)
    return jax.shard_map(
        body, mesh=mesh, in_specs=in_specs, out_specs=out_specs, check_vma=False
    )
```

time: 470 us -> 416 us (0.89)
  waiting for transfers between devices: 357 us -> 179 us
  Pallas kernels: 0 us -> 160 us
  matrix products: 60.8 us -> 16.9 us
  local copies, waits for them, and re-layouts: 10.6 us -> 32.5 us
  other arithmetic: 26.4 us -> 12.1 us
    all_gather x5 -> x2, waiting for transfers between devices: 284 us -> 98 us  [the longest x1 50.2 us: fast_device(): weight_all = lax.all_gather(out_weight, 'row', axis=0, tiled=True)]
    pallas_call x0 -> x2, Pallas kernels: none -> 160 us  [the longest x1 114 us: attention_fast(): pl.pallas_call(functools.partial(project_kernel, ncol), out_shape=jax.Sha...]
    dot_general x6 -> x2, matrix products: 60.8 us -> 16.9 us  [the longest x1 9.4 us: fast_device(): jnp.einsum('tk,td->kd', whole_attn, grad_out, preferred_element_type=jnp....]
    reduce_sum x1 -> x0, other arithmetic: 13 us -> none  [per_device(): denom = jnp.sum(expo, axis=-1)]
    reshape x0 -> x3, local copies, waits for them, and re-layouts: none -> 12.9 us  [the longest x1 6.61 us: attention_fast(): normed = normed.reshape(tok_rows, nrow, depth).transpose(1, 0, 2)]
    ppermute x0 -> x1, waiting for transfers between devices: none -> 7.85 us  [fast_device(): got = lax.ppermute(give, 'row', [(i, i ^ 2) for i in range(nrow)])]
    unnamed x14 -> x18, local copies, waits for them, and re-layouts: 7.08 us -> 14.7 us
  transfers between devices with their start and end apart: 6 -> 4, of which waited for: 6 -> 4; matrix products, arithmetic and copies ran while one was open for 11% -> 4% of each run, Pallas kernels for 0% -> 0%
where the time goes in v1:
time: 416 us; the launch traced here: 415 us
  waiting for transfers between devices  179 us (43%)
  Pallas kernels  160 us (38%)
  local copies, waits for them, and re-layouts  32.5 us (8%)
  matrix products  16.9 us (4%)
  between operations  13.9 us (3%)
  other arithmetic  12.1 us (3%)
    pallas_call x1, Pallas kernels, attention_fast(): pl.pallas_call(functools.partial(project_kernel, ncol), out_shape=jax.Sha...  114 us
    reduce_scatter x1, waiting for transfers between devices, fast_device(): lax.psum_scatter(partial.astype(jnp.bfloat16), 'row', scatter_dimension=0...  72.6 us
    all_gather x1, waiting for transfers between devices, fast_device(): weight_all = lax.all_gather(out_weight, 'row', axis=0, tiled=True)  50.2 us
    all_gather x1, waiting for transfers between devices, fast_device(): whole_attn = lax.all_gather(attn_here, 'col', axis=1, tiled=True)  47.8 us
    pallas_call x1, Pallas kernels, attention_fast(): pl.pallas_call(attend_kernel, out_shape=jax.ShapeDtypeStruct((2 * tok_row...  45.7 us
    unnamed x18, local copies, waits for them, and re-layouts  14.7 us
    dot_general x1, matrix products, fast_device(): jnp.einsum('tk,td->kd', whole_attn, grad_out, preferred_element_type=jnp....  9.4 us
  transfers between devices with their start and end apart: 4, of which 4 were waited for; matrix products, arithmetic and copies ran while one was open for 4% of the time, Pallas kernels for 0%

profile of v1, /device:TPU:0, one launch (start us, length us, event | category | flops | bytes accessed | tf_op | source)
XLA Modules:
  0.0 415.4 jit_solution(11114495167782620724)
XLA Ops:
  7.2 0.0 copy-start
  7.2 0.0 all-gather.3.cloned.1.call-start
  7.3 6.7 %copy.14 = bf16[384,6144]{0,1:T(8,128)(2,1)} copy(bf16[384,6144]{1,0:T(8,128)(2,1)} %param.8) | data formatting | bytes 9437184 | tf_op args[0]
  14.0 0.0 copy-start.2
  14.0 0.0 copy-start.3
  14.0 3.3 convert_reduce_fusion
  17.3 0.4 copy-done.2
  17.7 1.3 fusion.2
  19.0 0.0 copy-done.3
  19.0 3.4 fusion.4
  22.5 6.6 %copy.15 = bf16[384,8,768]{2,0,1:T(8,128)(2,1)} copy(bf16[384,8,768]{0,2,1:T(8,128)(2,1)} %bitcast.16) | data formatting | bytes 9437184 | tf_op jit(solution)/shard_map/reshape | solution.py:270
  29.1 6.1 %copy.16 = bf16[768,3,768]{0,2,1:T(8,128)(2,1)} copy(bf16[768,3,768]{2,0,1:T(8,128)(2,1)} %param.10) | data formatting | bytes 7077888 | tf_op args[2]
  35.2 4.0 copy.17
  39.2 0.0 copy-start.4
  39.2 0.0 copy-start.5
  39.2 0.0 copy-start.6
  39.2 5.9 %copy.18.w_ref = bf16[2,768,1152]{2,1,0:T(8,128)(2,1)} copy(bf16[2,768,1152]{1,2,0:T(8,128)(2,1)} %bitcast.18) | data formatting | bytes 7077888 | tf_op jit(solution)/shard_map/reshape | solution.py:272
  45.1 0.0 copy-done.4
  45.1 0.4 reshape.45
  45.6 0.1 select_n.82
  45.8 0.0 copy-done.5
  45.8 0.0 copy-done.6
  45.8 0.6 constant_dynamic-slice_fusion.2
  46.4 114.2 %project.1.qkv_ref = bf16[3,3,768,128]{3,2,1,0:T(8,128)(2,1)} custom-call(bf16[8,384,768]{2,1,0:T(8,128)(2,1)} %bitcast.17, bf16[2,768,1152]{2,1,0:T(8,128)(2,1)} %copy.18.w_ref, f32[3,128]{1,0:T(4,128)} %get-tuple-element.9.qg_ref, f32[3,128]{1,0:T(4,128)} %get-tuple-element.8.kg_ref), custom_call_target="tpu_custom_call" | custom-call | tf_op jit(solution)/shard_map/project/pallas_call | solution.py:276
  160.6 0.1 broadcast_in_dim.16
  160.7 0.0 copy-start.1
  160.7 1.5 copy-done.1
  162.2 45.7 %attend.1 = bf16[768,384]{1,0:T(8,128)(2,1)S(1)} custom-call(bf16[3,3,768,128]{3,2,1,0:T(8,128)(2,1)S(1)} %copy-done.1, f32[3,6,1,3072]{3,2,1,0:T(1,128)S(1)} %bitcast.15), custom_call_target="tpu_custom_call" | custom-call | tf_op jit(solution)/shard_map/attend/pallas_call | solution.py:301
  207.9 0.6 collective-permute-start
  208.6 7.8 %collective-permute-done = bf16[384,384]{1,0:T(8,128)(2,1)S(1)} collective-permute-done((bf16[384,384]{1,0:T(8,128)(2,1)S(1)}, bf16[384,384]{1,0:T(8,128)(2,1)S(1)}, u32[]{:S(2)}, u32[]{:S(2)}) %collective-permute-start) | collective-permute-done | bytes 294944 | tf_op jit(solution)/shard_map/ppermute | solution.py:325
  216.4 0.1 broadcast_select_fusion.1
  216.6 0.9 pad_maximum_fusion
  217.4 0.0 all-gather.3.cloned.1.call-update
  217.4 0.0 all-gather.5.cloned.1.call-start
  217.5 0.7 all-gather.5.cloned.1.call-update
  218.2 0.3 reduce-scatter.2.cloned.1.call-start
  218.5 47.8 %all-gather.3.cloned.1.call-done = bf16[384,3072]{1,0:T(8,128)(2,1)} async-done(((bf16[384,768]{1,0:T(8,128)(2,1)}), bf16[384,3072]{1,0:T(8,128)(2,1)}) %all-gather.3.cloned.1.call-update) | async-done | bytes 2359312 | tf_op jit(solution)/shard_map/all_gather | solution.py:329
  266.3 0.0 copy-done
  266.3 9.4 %convolution_convert_fusion = bf16[3072,1536]{1,0:T(8,128)(2,1)} fusion(bf16[384,3072]{1,0:T(8,128)(2,1)} %all-gather.3.cloned.1.call-done, bf16[384,1536]{1,0:T(8,128)(2,1)S(1)} %copy-done), kind=kOutput, calls=%fused_computation.2 | convolution fusion | flops 3628597248 | bytes 12976128 | tf_op jit(solution)/shard_map/tk,td->kd/dot_general | solution.py:330
  275.7 0.0 copy-start.7
  275.7 0.0 reduce-scatter.2.cloned.1.call-update
  275.7 50.2 %all-gather.5.cloned.1.call-done = bf16[3072,1536]{1,0:T(8,128)(2,1)} async-done(((bf16[384,1536]{1,0:T(8,128)(2,1)}), bf16[3072,1536]{1,0:T(8,128)(2,1)}) %all-gather.5.cloned.1.call-update) | async-done | bytes 9437200 | tf_op jit(solution)/shard_map/all_gather | solution.py:322
  325.9 0.0 copy-done.7
  325.9 7.5 %convolution_convert_fusion.1 = bf16[384,1536]{1,0:T(8,128)(2,1)} fusion(bf16[384,3072]{1,0:T(8,128)(2,1)S(1)} %copy-done.7, bf16[3072,1536]{1,0:T(8,128)(2,1)} %all-gather.5.cloned.1.call-done), kind=kOutput, calls=%fused_computation.8 | convolution fusion | flops 3624468480 | bytes 12976128 | tf_op jit(solution)/shard_map/dot_general | solution.py:334
  333.3 72.6 %reduce-scatter.2.cloned.1.call-done = bf16[384,1536]{1,0:T(8,128)(2,1)} async-done(((bf16[3072,1536]{1,0:T(8,128)(2,1)}), bf16[384,1536]{1,0:T(8,128)(2,1)}) %reduce-scatter.2.cloned.1.call-update) | async-done | bytes 1179664 | tf_op jit(solution)/shard_map/reduce_scatter | solution.py:331
  405.9 3.0 convert_element_type.19
  (6 shorter events, 0.1 us)
Async XLA Ops:
  7.2 259.1 %copy-start = (bf16[384,1536]{1,0:T(8,128)(2,1)S(1)}, bf16[384,1536]{1,0:T(8,128)(2,1)}, u32[]{:S(2)}) copy-start(bf16[384,1536]{1,0:T(8,128)(2,1)} %param.15) | copy-start | bytes 3538948
  7.2 259.1 %all-gather.3.cloned.1.call-start = ((), (), s32[]{:S(2)}) async-start(), calls=%async_computation.1 | async-start | bytes 2949120 | tf_op jit(solution)/shard_map/all_gather | solution.py:329
  14.0 3.8 copy-start.2
  14.0 5.1 %copy-start.3 = (f32[6144]{0:T(1024)S(1)}, f32[6144]{0:T(1024)}, u32[]{:S(2)}) copy-start(f32[6144]{0:T(1024)} %param.9) | copy-start | bytes 73732
  39.2 5.9 %copy-start.4 = (s32[6,24,24]{2,1,0:T(8,128)S(1)}, s32[6,24,24]{2,1,0:T(8,128)}, u32[]{:S(2)}) copy-start(s32[6,24,24]{2,1,0:T(8,128)} %param.13) | copy-start | bytes 41476
  39.2 6.6 %copy-start.5 = (f32[6,128]{1,0:T(8,128)S(1)}, f32[6,128]{1,0:T(8,128)}, u32[]{:S(2)}) copy-start(f32[6,128]{1,0:T(8,128)} %param.12) | copy-start | bytes 9220
  39.2 6.6 %copy-start.6 = (f32[6,128]{1,0:T(8,128)S(1)}, f32[6,128]{1,0:T(8,128)}, u32[]{:S(2)}) copy-start(f32[6,128]{1,0:T(8,128)} %param.11) | copy-start | bytes 9220
  160.7 1.5 copy-start.1
  207.9 8.5 %collective-permute-start = (bf16[384,384]{1,0:T(8,128)(2,1)S(1)}, bf16[384,384]{1,0:T(8,128)(2,1)S(1)}, u32[]{:S(2)}, u32[]{:S(2)}) collective-permute-start(bf16[384,384]{1,0:T(8,128)(2,1)S(1)} %constant_dynamic-slice_fusion), channel_id=1, source_target_pairs={{0,8},{4,12},{8,0},{12,4},{16,24},{20,28},{24,16},{28,20},{1,9},{5... | collective-permute-start | bytes 884744 | tf_op jit(solution)/shard_map/ppermute | solution.py:325
  217.4 108.4 %all-gather.5.cloned.1.call-start = ((), (), s32[]{:S(2)}) async-start(), calls=%async_computation.2 | async-start | bytes 10616832 | tf_op jit(solution)/shard_map/all_gather | solution.py:322
  218.2 187.7 %reduce-scatter.2.cloned.1.call-start = ((), (), s32[]{:S(2)}) async-start(), calls=%async_computation.3 | async-start | bytes 10616832 | tf_op jit(solution)/shard_map/reduce_scatter | solution.py:331
  275.7 50.2 %copy-start.7 = (bf16[384,3072]{1,0:T(8,128)(2,1)S(1)}, bf16[384,3072]{1,0:T(8,128)(2,1)}, u32[]{:S(2)}) copy-start(bf16[384,3072]{1,0:T(8,128)(2,1)} %all-gather.3.cloned.1.call-done) | copy-start | bytes 7077892
Sparse Core Ops, SparseCore 0:
  217.6 48.6 all-gather.2
  268.2 57.6 all-gather.4
  329.4 76.4 reduce-scatter.1

commit v2 on v1

--- a/solution.py
+++ b/solution.py
@@ -40,10 +40,9 @@
                    w_recv, w_send, t_recv, t_send):
     row, col, mate, xn, yn, dn = places()
     half = (row // 2) % 2
-    rows_tok, depth = tok_ref.shape[1], tok_ref.shape[2]
-    per = tok_ref.shape[0] // ncol
-    width = w_ref.shape[-1]
-    tile = width // 3
+    rows_tok, depth = tbuf.shape[1], tbuf.shape[2]
+    per = tbuf.shape[0] // ncol
+    tile = w_ref.shape[-1]
     sub = depth // SUBS
 
     barrier = pltpu.get_barrier_semaphore()
@@ -61,10 +60,13 @@
     pl.semaphore_wait(barrier, 3 + jnp.where(col > 0, 1, 0) + jnp.where(col < ncol - 1, 1, 0))
 
     def wpart(block, s):
-        return wbuf.at[block, pl.ds(s * sub, sub)]
+        return wbuf.at[block, :, pl.ds(s * sub, sub)]
 
     def wown(which, s):
-        return w_ref.at[which, pl.ds(s * sub, sub)]
+        return w_ref.at[which, :, pl.ds(s * sub, sub)]
+
+    def mine(block):
+        return tok_ref.at[:, pl.ds(pl.multiple_of(block * depth, depth), depth)]
 
     def wcopy(src, block, s, slot, device):
         return remote(src, wpart(block, s), w_send.at[slot, s], w_recv.at[block, s], (device, col))
@@ -72,7 +74,7 @@
     def tcopy(src, block, q, slot, device):
         return remote(src, tbuf.at[block], t_send.at[slot, q], t_recv.at[block], device)
 
-    first = [tcopy(tok_ref.at[col * per + q], col * per + q, q, 0, (xn, col)) for q in range(per)]
+    first = [tcopy(mine(col * per + q), col * per + q, q, 0, (xn, col)) for q in range(per)]
     for copy in first:
         copy.start()
     to_y = [wcopy(wown(half, s), row, s, 0, yn) for s in range(SUBS)]
@@ -88,13 +90,13 @@
         @pl.loop(0, 3)
         def _(t):
             cols = pl.ds(pl.multiple_of(t * tile, tile), tile)
-            prod = jnp.dot(left[...], right[:, cols], preferred_element_type=jnp.float32)
+            prod = jnp.dot(left[...], right[t], preferred_element_type=jnp.float32)
             if fresh:
                 acc[pl.ds(at, rows_tok), cols] = prod
             else:
                 acc[pl.ds(at, rows_tok), cols] += prod
 
-    times(own_at, tok_ref.at[row], w_ref.at[half], True)
+    times(own_at, mine(row), w_ref.at[half], True)
 
     def up(block, q, slot):
         return tcopy(tbuf.at[block], block, q, slot, (row, col + 1))
@@ -157,19 +159,19 @@
     spread(1, 0)
     pass_w(yn, 1, [(3, mate)])
     spread(1, 1)
-    times(own_at, tok_ref.at[yn], wbuf.at[yn], False)
+    times(own_at, mine(yn), wbuf.at[yn], False)
     pass_w(xn, 0, [(4, yn), (5, mate)])
     spread(2, 0)
     pass_w(xn, 1, [(4, yn), (5, mate)])
     spread(2, 1)
-    times(own_at, tok_ref.at[xn], wbuf.at[xn], False)
+    times(own_at, mine(xn), wbuf.at[xn], False)
     for block in (mate, flip(mate, 4), flip(mate, 2)):
         for s in range(SUBS):
             w_got(block, s)
-        times(own_at, tok_ref.at[block], wbuf.at[block], False)
+        times(own_at, mine(block), wbuf.at[block], False)
     for s in range(SUBS):
         pass_w(dn, s, [(6, mate)])
-    times(own_at, tok_ref.at[dn], wbuf.at[dn], False)
+    times(own_at, mine(dn), wbuf.at[dn], False)
     for dist in range(3, ncol):
         for q in range(per):
             spread(dist, q)
@@ -179,7 +181,7 @@
     last = flip(dn, 1)
     for s in range(SUBS):
         w_got(last, s)
-    times(own_at, tok_ref.at[last], wbuf.at[last], False)
+    times(own_at, mine(last), wbuf.at[last], False)
     times(nbr_at, tbuf.at[last], wbuf.at[last], False)
 
     heads = qg_ref.shape[0]
@@ -206,38 +208,107 @@
                 down(block, q, 2 * dist + 2).wait_send()
 
 
-def attend_kernel(qkv_ref, bias_ref, out_ref, kvbuf, recv, send):
+def attend_kernel(ncol, qkv_ref, bias_ref, ow_ref, grad_ref, out_ref, dw_ref,
+                  kvbuf, stage, abuf, owbuf, turned, msend, mrecv, dsend, s2, r1, r2,
+                  kv_recv, kv_send, ow_recv, ow_send, a_recv, a_send, x_send,
+                  m_recv, m_send, r1_recv, r1_send, r2_recv, r2_send):
     row, col, mate, xn, yn, dn = places()
+    half = (row // 2) % 2
     heads, rows = qkv_ref.shape[1], qkv_ref.shape[2]
+    toks = rows // 2
     here = 2 * (row // 4) + row % 2
     yslot = flip(here, 2)
     barrier = pltpu.get_barrier_semaphore()
-    for other in (mate, yn):
+    for other in (mate, xn, yn):
         pl.semaphore_signal(barrier, inc=1, device_id=(other, col), device_id_type=MESH)
-    pl.semaphore_wait(barrier, 2)
-
-    def copy(src, kv, h, slot, way, device):
-        return remote(src, kvbuf.at[kv, h, slot], send.at[way, kv, h], recv.at[kv, h, slot], (device, col))
-
+
+    @pl.when(col > 0)
+    def _():
+        pl.semaphore_signal(barrier, inc=1, device_id=(row, col - 1), device_id_type=MESH)
+
+    @pl.when(col < ncol - 1)
+    def _():
+        pl.semaphore_signal(barrier, inc=1, device_id=(row, col + 1), device_id_type=MESH)
+
+    pl.semaphore_wait(barrier, 3 + jnp.where(col > 0, 1, 0) + jnp.where(col < ncol - 1, 1, 0))
     started = []
+
+    def go(copy):
+        copy.start()
+        started.append(copy)
+
+    def kv_copy(src, kv, h, slot, way, device):
+        return remote(src, kvbuf.at[kv, h, slot], kv_send.at[way, kv, h], kv_recv.at[kv, h, slot], (device, col))
+
+    cut = ow_ref.shape[0] // 2
+
+    def ow_at(block, s):
+        return owbuf.at[block, pl.ds(s * cut, cut)]
+
+    def ow_copy(src, block, s, way, device):
+        return remote(src, ow_at(block, s), ow_send.at[way, s], ow_recv.at[block, s], (device, col))
+
+    def ow_own(s):
+        return ow_ref.at[pl.ds(s * cut, cut)]
+
+    def ow_pass(block, s, ways):
+        ow_copy(ow_at(block, s), block, s, 0, xn).wait_recv()
+        for way, device in ways:
+            go(ow_copy(ow_at(block, s), block, s, way, device))
+
     for h in range(heads):
         for kv in range(2):
             for way, device in ((0, yn), (1, mate)):
-                one = copy(qkv_ref.at[1 + kv, h], kv, h, here, way, device)
-                one.start()
-                started.append(one)
+                go(kv_copy(qkv_ref.at[1 + kv, h], kv, h, here, way, device))
             kvbuf[kv, h, here] = qkv_ref[1 + kv, h]
+    for s in range(2):
+        go(ow_copy(ow_own(s), row, s, 0, xn))
+    owbuf[row] = ow_ref[...]
+    for h in range(heads):
+        for kv in range(2):
+            kv_copy(kvbuf.at[kv, h, yslot], kv, h, yslot, 2, mate).wait_recv()
+            go(kv_copy(kvbuf.at[kv, h, yslot], kv, h, yslot, 2, mate))
+    for s in range(2):
+        go(ow_copy(ow_own(s), row, s, 1, yn))
+        go(ow_copy(ow_own(s), row, s, 2, mate))
+
+    def a_copy(src, p, way, device):
+        return remote(src, abuf.at[p], a_send.at[way, p], a_recv.at[p], device)
+
+    def a_up(p):
+        return a_copy(abuf.at[p], p, 0, (row, col + 1))
+
+    def a_down(p):
+        return a_copy(abuf.at[p], p, 1, (row, col - 1))
+
+    def a_got(p):
+        a_copy(abuf.at[p], p, 0, (xn, col)).wait_recv()
+
+    def piece(plane, other, h):
+        side = half + other - 2 * half * other
+        return (2 * plane + side) * heads + h
+
+    def z_out(p):
+        @pl.when(col < ncol - 1)
+        def _():
+            a_up(p).start()
+
+        @pl.when(col > 0)
+        def _():
+            a_down(p).start()
+
+    def x_got(h):
+        p = piece(col, 1, h)
+        a_got(p)
+        z_out(p)
+
+    own_at = pl.ds(pl.multiple_of(half * toks, toks), toks)
+    nbr_at = pl.ds(pl.multiple_of((1 - half) * toks, toks), toks)
     scale = HS ** (-0.5)
     for h in range(heads):
         for kv in range(2):
-            copy(kvbuf.at[kv, h, yslot], kv, h, yslot, 2, mate).wait_recv()
-            one = copy(kvbuf.at[kv, h, yslot], kv, h, yslot, 2, mate)
-            one.start()
-            started.append(one)
-    for h in range(heads):
-        for kv in range(2):
-            copy(kvbuf.at[kv, h, 0], kv, h, flip(here, 1), 2, mate).wait_recv()
-            copy(kvbuf.at[kv, h, 0], kv, h, flip(yslot, 1), 2, mate).wait_recv()
+            kv_copy(kvbuf.at[kv, h, 0], kv, h, flip(here, 1), 2, mate).wait_recv()
+            kv_copy(kvbuf.at[kv, h, 0], kv, h, flip(yslot, 1), 2, mate).wait_recv()
 
         @pl.loop(0, rows // BLOCK)
         def _(b):
@@ -251,25 +322,150 @@
             denom = jnp.sum(expo, axis=-1, keepdims=True)
             prod = jnp.dot(expo.astype(jnp.bfloat16), kvbuf[1, h].reshape(4 * rows, HS),
                            preferred_element_type=jnp.float32)
-            out_ref[at, h * HS:(h + 1) * HS] = (prod / denom).astype(jnp.bfloat16)
-    for one in started:
-        one.wait_send()
+            stage[h, at, :] = (prod / denom).astype(jnp.bfloat16)
+
+        p = piece(col, 0, h)
+        go(remote(stage.at[h, nbr_at], abuf.at[p], x_send.at[h], a_recv.at[p], (xn, col)))
+        abuf[p] = stage[h, own_at, :]
+        z_out(p)
+        if h >= 1:
+            x_got(h - 1)
+        if h == 0:
+            ow_pass(xn, 0, [(3, yn), (4, mate)])
+            ow_pass(xn, 1, [(4, mate)])
+    x_got(heads - 1)
+    ow_pass(yn, 0, [(5, mate)])
+    ow_pass(yn, 1, [(3, xn), (5, mate)])
+    order = [(0, 0), (0, 1), (1, 0), (0, 2), (1, 1), (1, 2)]
+    for dist in range(1, ncol):
+        for other, h in order:
+            @pl.when(col >= dist)
+            def _():
+                p = piece(col - dist, other, h)
+                a_got(p)
+
+                @pl.when(col < ncol - 1)
+                def _():
+                    a_up(p).start()
+
+            @pl.when(col + dist < ncol)
+            def _():
+                p = piece(col + dist, other, h)
+                a_got(p)
+
+                @pl.when(col > 0)
+                def _():
+                    a_down(p).start()
+        if dist == 1:
+            for s in range(2):
+                ow_pass(dn, s, [(6, mate)])
+
+    wide = ow_ref.shape[1]
+    tile = wide // 3
+
+    def turn(block):
+        turned[...] = jnp.concatenate([abuf[3 * block + i] for i in range(3)], axis=1).T
+
+    def tiles(body):
+        @pl.loop(0, 3)
+        def _(t):
+            body(pl.ds(pl.multiple_of(t * tile, tile), tile))
+
+    def grad_tile(cols):
+        return jnp.dot(turned[...], grad_ref[:, cols], preferred_element_type=jnp.float32)
+
+    blocks = (dn, xn, yn, row)
+
+    def m_copy(i):
+        return remote(msend.at[i], mrecv.at[i], m_send.at[i], m_recv.at[i], (mate, col))
+
+    for i, block in enumerate(blocks):
+        turn(flip(block, 1))
+
+        def to_mate(cols):
+            msend[i, :, cols] = grad_tile(cols).astype(jnp.bfloat16)
+
+        tiles(to_mate)
+        go(m_copy(i))
+
+    def r1_copy(i, side, through, device):
+        return remote(dsend.at[i, pl.ds(side * cut, cut)], r1.at[side, through], r1_send.at[side, through],
+                      r1_recv.at[side, through], (device, col))
+
+    def r2_copy(side, device):
+        return remote(s2.at[side], r2.at[side], r2_send.at[side], r2_recv.at[side], (device, col))
+
+    for i, block in enumerate(blocks):
+        turn(block)
+        m_copy(i).wait_recv()
+
+        def total(cols):
+            both = grad_tile(cols) + mrecv[i, :, cols].astype(jnp.float32)
+            if i < 3:
+                dsend[i, :, cols] = both.astype(jnp.bfloat16)
+            else:
+                dw_ref[:, cols] = both
+
+        tiles(total)
+        if i == 0:
+            go(r1_copy(0, 0, 1, xn))
+            go(r1_copy(0, 1, 1, yn))
+        elif i == 1:
+            go(r1_copy(1, 0, 0, xn))
+        elif i == 2:
+            go(r1_copy(2, 1, 0, yn))
+    for side, i, source, target in ((1, 1, yn, xn), (0, 2, xn, yn)):
+        r1_copy(0, side, 1, source).wait_recv()
+        held = dsend[i, side * cut:(side + 1) * cut, :].astype(jnp.float32)
+        s2[side] = (held + r1[side, 1].astype(jnp.float32)).astype(jnp.bfloat16)
+        go(r2_copy(side, target))
+
+    for block in (mate, flip(xn, 1), flip(yn, 1), flip(dn, 1)):
+        for s in range(2):
+            ow_copy(ow_at(block, s), block, s, 0, mate).wait_recv()
+
+    def project(cols):
+        sums = jnp.zeros((toks, tile), jnp.float32)
+        for plane in range(ncol):
+            left = jnp.concatenate([abuf[2 * heads * plane + i] for i in range(2 * heads)], axis=1)
+            right = owbuf[2 * plane:2 * plane + 2, :, cols].reshape(4 * cut, tile)
+            sums += jnp.dot(left, right, preferred_element_type=jnp.float32)
+        out_ref[:, cols] = sums.astype(jnp.bfloat16)
+
+    tiles(project)
+    for side, near, far in ((0, xn, yn), (1, yn, xn)):
+        r1_copy(0, side, 0, near).wait_recv()
+        r2_copy(side, far).wait_recv()
+        at = slice(side * cut, (side + 1) * cut)
+        dw_ref[at, :] += r1[side, 0].astype(jnp.float32) + r2[side].astype(jnp.float32)
+
+    for copy in started:
+        copy.wait_send()
+    for dist in range(ncol):
+        for other, h in order:
+            @pl.when((col >= dist) & (col < ncol - 1))
+            def _():
+                a_up(piece(col - dist, other, h)).wait_send()
+
+            @pl.when((col + dist < ncol) & (col > 0))
+            def _():
+                a_down(piece(col + dist, other, h)).wait_send()
 
 
 def vmem(count):
     return [pl.BlockSpec(memory_space=pltpu.VMEM)] * count
 
 
-def attention_fast(ncol, nrow, tokens, ln_gain, qkv_weight, q_gain, k_gain, block_mask):
+def fast_device(ncol, nrow, tokens, ln_gain, qkv_weight, q_gain, k_gain, block_mask, out_weight, grad_out):
     tok_rows, feats = tokens.shape
     depth, _, col_width = qkv_weight.shape
     heads = q_gain.shape[0] // 2
     row = lax.axis_index("row")
     half = (row // 2) % 2
     normed = norm_rows(tokens.astype(jnp.float32), ln_gain).astype(jnp.bfloat16)
-    normed = normed.reshape(tok_rows, nrow, depth).transpose(1, 0, 2)
     wide = 3 * heads * HS
-    weight = qkv_weight.reshape(depth, 3, 2, heads * HS).transpose(2, 0, 1, 3).reshape(2, depth, wide)
+    by_kind = qkv_weight.transpose(1, 0, 2)
+    weight = jnp.stack([by_kind[:, :, :heads * HS], by_kind[:, :, heads * HS:]])
     qg = lax.dynamic_slice_in_dim(q_gain, half * heads, heads, 0)
     kg = lax.dynamic_slice_in_dim(k_gain, half * heads, heads, 0)
     dma = pltpu.SemaphoreType.DMA
@@ -279,7 +475,7 @@
         in_specs=vmem(4),
         out_specs=vmem(1)[0],
         scratch_shapes=[
-            pltpu.VMEM((nrow, depth, wide), jnp.bfloat16),
+            pltpu.VMEM((nrow, 3, depth, heads * HS), jnp.bfloat16),
             pltpu.VMEM((nrow, tok_rows, depth), jnp.bfloat16),
             pltpu.VMEM((2 * tok_rows, wide), jnp.float32),
             dma((nrow, SUBS)), dma((7, SUBS)), dma((nrow,)), dma((2 * ncol + 1, nrow // ncol)),
@@ -298,41 +494,34 @@
     mine = mine.transpose(0, 1, 2, 3, 5, 4, 6).reshape(heads, 2 * per, nblocks)
     bias = jnp.where(mine > 0, 0.0, -1e30).astype(jnp.float32)
     bias = jnp.repeat(bias, BLOCK, axis=2).reshape(heads, 2 * per, 1, nblocks * BLOCK)
-    return pl.pallas_call(
-        attend_kernel,
-        out_shape=jax.ShapeDtypeStruct((2 * tok_rows, heads * HS), jnp.bfloat16),
-        in_specs=vmem(2),
-        out_specs=vmem(1)[0],
+    half_rows, out_wide = out_weight.shape[0] // 2, out_weight.shape[1]
+    bf = jnp.bfloat16
+    return tuple(pl.pallas_call(
+        functools.partial(attend_kernel, ncol),
+        out_shape=[jax.ShapeDtypeStruct((tok_rows, out_wide), bf),
+                   jax.ShapeDtypeStruct(out_weight.shape, jnp.float32)],
+        in_specs=vmem(4),
+        out_specs=vmem(2),
         scratch_shapes=[
-            pltpu.VMEM((2, heads, 4, 2 * tok_rows, HS), jnp.bfloat16),
-            dma((2, heads, 4)), dma((3, 2, heads)),
+            pltpu.VMEM((2, heads, 4, 2 * tok_rows, HS), bf),
+            pltpu.VMEM((heads, 2 * tok_rows, HS), bf),
+            pltpu.VMEM((2 * ncol * heads, tok_rows, HS), bf),
+            pltpu.VMEM((nrow, *out_weight.shape), bf),
+            pltpu.VMEM((heads * HS, tok_rows), bf),
+            pltpu.VMEM((4, *out_weight.shape), bf),
+            pltpu.VMEM((4, *out_weight.shape), bf),
+            pltpu.VMEM((3, *out_weight.shape), bf),
+            pltpu.VMEM((2, half_rows, out_wide), bf),
+            pltpu.VMEM((2, 2, half_rows, out_wide), bf),
+            pltpu.VMEM((2, half_rows, out_wide), bf),
+            dma((2, heads, 4)), dma((3, 2, heads)), dma((nrow, 2)), dma((7, 2)),
+            dma((2 * ncol * heads,)), dma((2, 2 * ncol * heads)), dma((heads,)),
+            dma((4,)), dma((4,)), dma((2, 2)), dma((2, 2)), dma((2,)), dma((2,)),
         ],
         compiler_params=pltpu.CompilerParams(
-            collective_id=1, has_side_effects=True, vmem_limit_bytes=48 * 2**20),
+            collective_id=1, has_side_effects=True, vmem_limit_bytes=60 * 2**20),
         name="attend",
-    )(qkv, bias)
-
-
-def fast_device(ncol, nrow, tokens, ln_gain, qkv_weight, q_gain, k_gain, block_mask, out_weight, grad_out):
-    tok_rows = tokens.shape[0]
-    row = lax.axis_index("row")
-    half = (row // 2) % 2
-    attn = attention_fast(ncol, nrow, tokens, ln_gain, qkv_weight, q_gain, k_gain, block_mask)
-    out_weight, attn = lax.optimization_barrier((out_weight, attn))
-    weight_all = lax.all_gather(out_weight, "row", axis=0, tiled=True)
-    own = lax.dynamic_slice_in_dim(attn, half * tok_rows, tok_rows, 0)
-    give = lax.dynamic_slice_in_dim(attn, (1 - half) * tok_rows, tok_rows, 0)
-    got = lax.ppermute(give, "row", [(i, i ^ 2) for i in range(nrow)])
-    first = jnp.where(half == 0, own, got)
-    second = jnp.where(half == 0, got, own)
-    attn_here = jnp.concatenate([first, second], axis=1)
-    whole_attn = lax.all_gather(attn_here, "col", axis=1, tiled=True)
-    partial = jnp.einsum("tk,td->kd", whole_attn, grad_out, preferred_element_type=jnp.float32)
-    weight_grad = lax.psum_scatter(
-        partial.astype(jnp.bfloat16), "row", scatter_dimension=0, tiled=True
-    ).astype(jnp.float32)
-    branch = jnp.dot(whole_attn, weight_all, preferred_element_type=jnp.float32)
-    return branch.astype(jnp.bfloat16), weight_grad
+    )(qkv, bias, out_weight, grad_out))
 
 
 def per_device(tokens, ln_gain, qkv_weight, q_gain, k_gain, block_mask, out_weight, grad_out):

time: 416 us -> 263 us (0.63)
  waiting for transfers between devices: 179 us -> 0 us
  Pallas kernels: 160 us -> 242 us
  local copies, waits for them, and re-layouts: 32.5 us -> 10.4 us
  matrix products: 16.9 us -> 0 us
  between operations: 13.9 us -> 0.81 us
    all_gather x2 -> x0, waiting for transfers between devices: 98 us -> none  [the longest x1 50.2 us: fast_device(): weight_all = lax.all_gather(out_weight, 'row', axis=0, tiled=True)]
    pallas_call x2, Pallas kernels: 160 us -> 242 us  [the longest x1 128 us: fast_device(): pl.pallas_call(functools.partial(attend_kernel, ncol), out_shape=[jax.Sha...]
    reduce_scatter x1 -> x0, waiting for transfers between devices: 72.6 us -> none  [fast_device(): lax.psum_scatter(partial.astype(jnp.bfloat16), 'row', scatter_dimension=0...]
    dot_general x2 -> x0, matrix products: 16.9 us -> none  [the longest x1 9.4 us: fast_device(): jnp.einsum('tk,td->kd', whole_attn, grad_out, preferred_element_type=jnp....]
    reshape x3 -> x1, local copies, waits for them, and re-layouts: 12.9 us -> 0.41 us  [fast_device(): order = mask.reshape(heads, 2, 2, 2, per, 2, 2, 2, per)]
    unnamed x18 -> x10, local copies, waits for them, and re-layouts: 14.7 us -> 5.34 us
    ppermute x1 -> x0, waiting for transfers between devices: 7.85 us -> none  [fast_device(): got = lax.ppermute(give, 'row', [(i, i ^ 2) for i in range(nrow)])]
  transfers between devices with their start and end apart: 4 -> 0, of which waited for: 4 -> 0; matrix products, arithmetic and copies ran while one was open for 4% -> 0% of each run, Pallas kernels for 0% -> 0%
where the time goes in v2:
time: 263 us
  Pallas kernels  242 us (92%)
  local copies, waits for them, and re-layouts  10.4 us (4%)
  other arithmetic  8.88 us (3%)
    pallas_call x1, Pallas kernels, fast_device(): pl.pallas_call(functools.partial(attend_kernel, ncol), out_shape=[jax.Sha...  128 us
    pallas_call x1, Pallas kernels, fast_device(): pl.pallas_call(functools.partial(project_kernel, ncol), out_shape=jax.Sha...  114 us
    unnamed x10, local copies, waits for them, and re-layouts  5.34 us

profile of v2, /device:TPU:0, one launch (start us, length us, event | category | flops | bytes accessed | tf_op | source)
XLA Modules:
  0.0 262.6 jit_solution(12833694720254059058)
XLA Ops:
  0.6 0.0 copy-start
  0.7 1.3 constant_dynamic-slice_fusion.1
  2.0 2.4 slice_bitcast_fusion.1
  4.3 0.0 copy-start.1
  4.4 2.2 pad_maximum_fusion.w_ref
  6.6 1.4 copy-done.1
  8.0 0.7 convert_reduce_fusion
  8.7 0.0 copy-start.3
  8.7 1.4 fusion.2
  10.1 0.0 copy-done.3
  10.1 4.5 %fusion.4.tok_ref = bf16[384,6144]{1,0:T(8,128)(2,1)} fusion(bf16[384,6144]{1,0:T(8,128)(2,1)S(1)} %copy-done.1, f32[6144]{0:T(1024)S(1)} %copy-done.3, f32[384]{0:T(512)S(1)} %add_rsqrt_fusion, f32[384]{0:T(512)S(1)} %broadcast_multiply_fusion), kind=kLoop, calls=%fused_computation.6 | loop fusion | flops 11796480 | bytes 9464832 | tf_op jit(solution)/shard_map/convert_element_type | solution.py:465
  14.6 114.2 %project.1.qkv_ref = bf16[3,3,768,128]{3,2,1,0:T(8,128)(2,1)} custom-call(bf16[384,6144]{1,0:T(8,128)(2,1)} %fusion.4.tok_ref, bf16[2,3,768,384]{3,2,1,0:T(8,128)(2,1)} %pad_maximum_fusion.w_ref, f32[3,128]{1,0:T(4,128)} %get-tuple-element.5.qg_ref, f32[3,128]{1,0:T(4,128)} %get-tuple-element.4.kg_ref), custom_call_target="tpu_custom_call" | custom-call | tf_op jit(solution)/shard_map/project/pallas_call | solution.py:472
  128.8 0.0 copy-done
  128.8 0.4 reshape.33
  129.4 0.1 select_n.60
  129.5 0.8 broadcast_in_dim.16
  130.4 128.3 %attend.1 = (bf16[384,1536]{1,0:T(8,128)(2,1)}, f32[384,1536]{1,0:T(8,128)}) custom-call(bf16[3,3,768,128]{3,2,1,0:T(8,128)(2,1)} %project.1.qkv_ref, f32[3,6,1,3072]{3,2,1,0:T(1,128)} %bitcast.11, bf16[384,1536]{1,0:T(8,128)(2,1)} %ow_ref.1, bf16[384,1536]{1,0:T(8,128)(2,1)} %grad_ref.1), custom_call_target="tpu_custom_call" | custom-call | tf_op jit(solution)/shard_map/attend/pallas_call | solution.py:499
  258.7 0.0 copy-start.2
  258.7 2.5 copy.13
  261.2 0.0 copy-done.2
  261.2 1.4 copy.14
  (5 shorter events, 0.1 us)
Async XLA Ops:
  0.6 128.2 %copy-start = (s32[6,24,24]{2,1,0:T(8,128)S(1)}, s32[6,24,24]{2,1,0:T(8,128)}, u32[]{:S(2)}) copy-start(s32[6,24,24]{2,1,0:T(8,128)} %param.13) | copy-start | bytes 41476
  4.3 3.6 %copy-start.1 = (bf16[384,6144]{1,0:T(8,128)(2,1)S(1)}, bf16[384,6144]{1,0:T(8,128)(2,1)}, u32[]{:S(2)}) copy-start(bf16[384,6144]{1,0:T(8,128)(2,1)} %param.8) | copy-start | bytes 14155780
  8.7 1.4 copy-start.3
  258.7 2.5 copy-start.2

commit v3 on v2

--- a/solution.py
+++ b/solution.py
@@ -42,7 +42,7 @@
     half = (row // 2) % 2
     rows_tok, depth = tbuf.shape[1], tbuf.shape[2]
     per = tbuf.shape[0] // ncol
-    tile = w_ref.shape[-1]
+    tile = wbuf.shape[-1]
     sub = depth // SUBS
 
     barrier = pltpu.get_barrier_semaphore()
@@ -63,7 +63,7 @@
         return wbuf.at[block, :, pl.ds(s * sub, sub)]
 
     def wown(which, s):
-        return w_ref.at[which, :, pl.ds(s * sub, sub)]
+        return w_ref.at[:, pl.ds(s * sub, sub), pl.ds(pl.multiple_of(which * tile, tile), tile)]
 
     def mine(block):
         return tok_ref.at[:, pl.ds(pl.multiple_of(block * depth, depth), depth)]
@@ -96,7 +96,9 @@
             else:
                 acc[pl.ds(at, rows_tok), cols] += prod
 
-    times(own_at, mine(row), w_ref.at[half], True)
+    wbuf[row] = w_ref[:, :, pl.ds(pl.multiple_of(half * tile, tile), tile)]
+    acc[pl.ds(nbr_at, rows_tok)] = jnp.zeros((rows_tok, acc.shape[1]), jnp.float32)
+    times(own_at, mine(row), wbuf.at[row], True)
 
     def up(block, q, slot):
         return tcopy(tbuf.at[block], block, q, slot, (row, col + 1))
@@ -169,20 +171,35 @@
         for s in range(SUBS):
             w_got(block, s)
         times(own_at, mine(block), wbuf.at[block], False)
+    def early(q):
+        return (q != dn // 2) & (q - col <= 2) & (col - q <= 2)
+
+    def quarter(q):
+        for i in range(per):
+            times(nbr_at, tbuf.at[per * q + i], wbuf.at[per * q + i], False)
+
+    @pl.loop(0, ncol)
+    def _(q):
+        @pl.when(early(q))
+        def _():
+            quarter(q)
+
     for s in range(SUBS):
         pass_w(dn, s, [(6, mate)])
     times(own_at, mine(dn), wbuf.at[dn], False)
     for dist in range(3, ncol):
         for q in range(per):
             spread(dist, q)
-    times(nbr_at, tbuf.at[row], w_ref.at[half], True)
-    for block in (mate, flip(mate, 4), flip(mate, 2), yn, xn, dn):
-        times(nbr_at, tbuf.at[block], wbuf.at[block], False)
     last = flip(dn, 1)
     for s in range(SUBS):
         w_got(last, s)
     times(own_at, mine(last), wbuf.at[last], False)
-    times(nbr_at, tbuf.at[last], wbuf.at[last], False)
+
+    @pl.loop(0, ncol)
+    def _(q):
+        @pl.when(jnp.logical_not(early(q)))
+        def _():
+            quarter(q)
 
     heads = qg_ref.shape[0]
     for kind in range(3):
@@ -336,30 +353,6 @@
     x_got(heads - 1)
     ow_pass(yn, 0, [(5, mate)])
     ow_pass(yn, 1, [(3, xn), (5, mate)])
-    order = [(0, 0), (0, 1), (1, 0), (0, 2), (1, 1), (1, 2)]
-    for dist in range(1, ncol):
-        for other, h in order:
-            @pl.when(col >= dist)
-            def _():
-                p = piece(col - dist, other, h)
-                a_got(p)
-
-                @pl.when(col < ncol - 1)
-                def _():
-                    a_up(p).start()
-
-            @pl.when(col + dist < ncol)
-            def _():
-                p = piece(col + dist, other, h)
-                a_got(p)
-
-                @pl.when(col > 0)
-                def _():
-                    a_down(p).start()
-        if dist == 1:
-            for s in range(2):
-                ow_pass(dn, s, [(6, mate)])
-
     wide = ow_ref.shape[1]
     tile = wide // 3
 
@@ -374,19 +367,55 @@
     def grad_tile(cols):
         return jnp.dot(turned[...], grad_ref[:, cols], preferred_element_type=jnp.float32)
 
-    blocks = (dn, xn, yn, row)
-
     def m_copy(i):
         return remote(msend.at[i], mrecv.at[i], m_send.at[i], m_recv.at[i], (mate, col))
 
-    for i, block in enumerate(blocks):
-        turn(flip(block, 1))
+    def mate_block(plane):
+        chip = row // 2
+        code = 2 * ((plane // 2 + chip // 2) % 2) + (plane + chip) % 2
+        i = jnp.where(code == 0, 3, jnp.where(code == 3, 0, code))
+        turn(2 * plane + 1 - row % 2)
 
         def to_mate(cols):
             msend[i, :, cols] = grad_tile(cols).astype(jnp.bfloat16)
 
         tiles(to_mate)
-        go(m_copy(i))
+        m_copy(i).start()
+
+    order = [(0, 0), (0, 1), (1, 0), (0, 2), (1, 1), (1, 2)]
+    mate_block(col)
+    for dist in range(1, ncol):
+        for other, h in order:
+            @pl.when(col >= dist)
+            def _():
+                p = piece(col - dist, other, h)
+                a_got(p)
+
+                @pl.when(col < ncol - 1)
+                def _():
+                    a_up(p).start()
+
+            @pl.when(col + dist < ncol)
+            def _():
+                p = piece(col + dist, other, h)
+                a_got(p)
+
+                @pl.when(col > 0)
+                def _():
+                    a_down(p).start()
+        @pl.when(col >= dist)
+        def _():
+            mate_block(col - dist)
+
+        @pl.when(col + dist < ncol)
+        def _():
+            mate_block(col + dist)
+
+        if dist == 1:
+            for s in range(2):
+                ow_pass(dn, s, [(6, mate)])
+
+    blocks = (dn, xn, yn, row)
 
     def r1_copy(i, side, through, device):
         return remote(dsend.at[i, pl.ds(side * cut, cut)], r1.at[side, through], r1_send.at[side, through],
@@ -441,6 +470,8 @@
 
     for copy in started:
         copy.wait_send()
+    for i in range(4):
+        m_copy(i).wait_send()
     for dist in range(ncol):
         for other, h in order:
             @pl.when((col >= dist) & (col < ncol - 1))
@@ -464,8 +495,7 @@
     half = (row // 2) % 2
     normed = norm_rows(tokens.astype(jnp.float32), ln_gain).astype(jnp.bfloat16)
     wide = 3 * heads * HS
-    by_kind = qkv_weight.transpose(1, 0, 2)
-    weight = jnp.stack([by_kind[:, :, :heads * HS], by_kind[:, :, heads * HS:]])
+    weight = qkv_weight.transpose(1, 0, 2)
     qg = lax.dynamic_slice_in_dim(q_gain, half * heads, heads, 0)
     kg = lax.dynamic_slice_in_dim(k_gain, half * heads, heads, 0)
     dma = pltpu.SemaphoreType.DMA

time: 263 us -> 252 us (0.958)
  Pallas kernels: 242 us -> 233 us
    pallas_call x1, Pallas kernels: 114 us -> 106 us  [fast_device(): pl.pallas_call(functools.partial(project_kernel, ncol), out_shape=jax.Sha...]
    unnamed x10 -> x8, local copies, waits for them, and re-layouts: 5.34 us -> 5.6 us
where the time goes in v3:
time: 252 us
  Pallas kernels  233 us (92%)
  other arithmetic  9.04 us (4%)
  local copies, waits for them, and re-layouts  8.47 us (3%)
    pallas_call x1, Pallas kernels, fast_device(): pl.pallas_call(functools.partial(attend_kernel, ncol), out_shape=[jax.Sha...  128 us
    pallas_call x1, Pallas kernels, fast_device(): pl.pallas_call(functools.partial(project_kernel, ncol), out_shape=jax.Sha...  106 us
    unnamed x8, local copies, waits for them, and re-layouts  5.6 us

profile of v3, /device:TPU:0, one launch (start us, length us, event | category | flops | bytes accessed | tf_op | source)
XLA Modules:
  0.0 251.5 jit_solution(1470800210759189642)
XLA Ops:
  0.6 0.0 copy-start
  0.7 0.0 copy-start.1
  0.7 1.4 constant_dynamic-slice_fusion.1
  2.1 0.0 copy-start.2
  2.1 3.1 %convert_reduce_fusion = f32[384]{0:T(512)S(1)} fusion(bf16[384,6144]{1,0:T(8,128)(2,1)} %param.8), kind=kLoop, calls=%fused_computation.1 | loop fusion | flops 4718208 | bytes 4720128 | tf_op jit(solution)/shard_map/reduce_sum | solution.py:18
  5.2 0.0 copy-done.1
  5.2 1.4 fusion.2
  6.6 0.0 copy-done.2
  6.6 4.6 %fusion.4.tok_ref = bf16[384,6144]{1,0:T(8,128)(2,1)} fusion(bf16[384,6144]{1,0:T(8,128)(2,1)S(1)} %copy-done.1, f32[6144]{0:T(1024)S(1)} %copy-done.2, f32[384]{0:T(512)S(1)} %add_rsqrt_fusion, f32[384]{0:T(512)S(1)} %broadcast_multiply_fusion), kind=kLoop, calls=%fused_computation.6 | loop fusion | flops 11796480 | bytes 9464832 | tf_op jit(solution)/shard_map/convert_element_type | solution.py:496
  11.2 105.6 %project.1.qkv_ref = bf16[3,3,768,128]{3,2,1,0:T(8,128)(2,1)} custom-call(bf16[384,6144]{1,0:T(8,128)(2,1)} %fusion.4.tok_ref, bf16[3,768,768]{2,1,0:T(8,128)(2,1)} %bitcast.6, f32[3,128]{1,0:T(4,128)} %get-tuple-element.3.qg_ref, f32[3,128]{1,0:T(4,128)} %get-tuple-element.2.kg_ref), custom_call_target="tpu_custom_call" | custom-call | tf_op jit(solution)/shard_map/project/pallas_call | solution.py:502
  116.8 0.0 copy-done
  116.8 0.4 reshape.33
  117.4 0.1 select_n.60
  117.5 0.8 broadcast_in_dim.16
  118.3 127.6 %attend.1 = (bf16[384,1536]{1,0:T(8,128)(2,1)}, f32[384,1536]{1,0:T(8,128)}) custom-call(bf16[3,3,768,128]{3,2,1,0:T(8,128)(2,1)} %project.1.qkv_ref, f32[3,6,1,3072]{3,2,1,0:T(1,128)} %bitcast.7, bf16[384,1536]{1,0:T(8,128)(2,1)} %ow_ref.1, bf16[384,1536]{1,0:T(8,128)(2,1)} %grad_ref.1), custom_call_target="tpu_custom_call" | custom-call | tf_op jit(solution)/shard_map/attend/pallas_call | solution.py:529
  245.9 2.4 copy.13
  248.3 3.2 %copy.14 = f32[384,1536]{1,0:T(8,128)} copy(f32[384,1536]{1,0:T(8,128)} %get-tuple-element.7) | data formatting | bytes 4718592
  (5 shorter events, 0.1 us)
Async XLA Ops:
  0.6 116.2 %copy-start = (s32[6,24,24]{2,1,0:T(8,128)S(1)}, s32[6,24,24]{2,1,0:T(8,128)}, u32[]{:S(2)}) copy-start(s32[6,24,24]{2,1,0:T(8,128)} %param.13) | copy-start | bytes 41476
  0.7 4.5 %copy-start.1 = (bf16[384,6144]{1,0:T(8,128)(2,1)S(1)}, bf16[384,6144]{1,0:T(8,128)(2,1)}, u32[]{:S(2)}) copy-start(bf16[384,6144]{1,0:T(8,128)(2,1)} %param.8) | copy-start | bytes 14155780
  2.1 4.5 %copy-start.2 = (f32[6144]{0:T(1024)S(1)}, f32[6144]{0:T(1024)}, u32[]{:S(2)}) copy-start(f32[6144]{0:T(1024)} %param.9) | copy-start | bytes 73732
